TPU v7x, 32 devices: a whole 2x2x4 slice. The times are simulated.
32 devices in a mesh: stream: 4 (over y, x), span: 8 (over z, core).
Axes of the slice: x: 2, y: 2, z: 4, core: 2. Of those that a mesh axis runs over, the one named last changes fastest.
Arguments:
- perturbation: float32 [5, 128, 512, 128], P(None, 'stream', 'span'), may hold values from -6 to 6
- base_flow: float32 [4, 128, 512, 128], P(None, 'stream', 'span'), may hold values from -1 to 1.2, as said below
- donor_stream: int32 [4, 2048], P('stream', 'span'), may hold values from 0 to 30
- donor_span: int32 [4, 2048], P('stream', 'span'), may hold values from 0 to 62
- donor_weights: float32 [3, 4, 2048], P(None, 'stream', 'span'), may hold values from 0 to 1
- donor_receiver: int32 [4, 2048], P('stream', 'span'), may hold values from 0 to 7, as said below
- target_stream: int32 [4, 2048], P('stream', 'span'), may hold values from 4 to 27
- target_span: int32 [4, 2048], P('stream', 'span'), may hold values from 4 to 59
Outputs:
- advanced: float32 [5, 128, 512, 128], P(None, 'stream', 'span')
Inputs may be any that keep to these rules, and one draw needn't show every extreme that they name: `donor_receiver`: in every streamwise row one spanwise block receives exactly 64 tiles from every block of the row, and no block sends more than 64 tiles to one receiving block. `base_flow`: component 0 lies in 0.4 to 1.2, component 1 in -0.4 to 0.4, component 2 in 0.5 to 1.0, component 3 in -1 to 1.
All inputs are finite; a program needn't handle non-finite values.
Results may differ from a plain program's by a relative error of at most 0.000073.
Values sent between devices are 32-bit elements; how exact they have to be, the bound alone decides.
A program may use at most 256 MiB of HBM per device.

v0:
```python
import functools

import jax
import jax.numpy as jnp
from jax import lax
from jax.experimental import pallas as pl
from jax.experimental.pallas import tpu as pltpu
from jax.sharding import PartitionSpec as P

viscosity = 0.02
penalty_rate = 1.5
time_step = 0.25
MESH = pl.DeviceIdType.MESH
F32 = jnp.float32
BF16 = jnp.bfloat16


def split(values):
    high = values.astype(BF16)
    low = (values - high.astype(F32)).astype(BF16)
    return high, low


def kernel(
    rows, spans, X, Z, donors, cap,
    pert, flow_in, meta, out,
    q, flow, send, recv, zsend, zrecv, tsend, trecv,
    a_high, a_low, wy, landing, counted, trow, qcat, band, ybuf,
    load_sem, out_sem, send_sem, recv_sem, xs_sem, xr_sem, zs_sem, zr_sem, ts_sem, tr_sem,
):
    sx = lax.axis_index("stream")
    me = lax.axis_index("span")
    Y = 128
    slots = spans * cap

    def load(f):
        return pltpu.make_async_copy(
            pert.at[f], q.at[0, f, pl.ds(2, X), pl.ds(8, Z), :], load_sem.at[f])

    flow_load = pltpu.make_async_copy(flow_in, flow, load_sem.at[5])
    for f in range(5):
        load(f).start()
    flow_load.start()

    barrier = pltpu.get_barrier_semaphore()
    for k in range(1, spans):
        pl.semaphore_signal(barrier, inc=1, device_id=(sx, lax.rem(me + k, spans)), device_id_type=MESH)

    for k in (1, rows - 1):
        pl.semaphore_signal(barrier, inc=1, device_id=(lax.rem(sx + k, rows), me), device_id_type=MESH)
    pl.semaphore_wait(barrier, spans + 1)

    @pl.when(sx == 0)
    def _():
        for s in range(3):
            for f in range(5):
                q[s, f, 0:2, 8:8 + Z, :] = jnp.zeros((2, Z, Y), F32)

    @pl.when(sx == rows - 1)
    def _():
        for s in range(3):
            for f in range(5):
                q[s, f, X + 2:X + 4, 8:8 + Z, :] = jnp.zeros((2, Z, Y), F32)

    r = lax.broadcasted_iota(jnp.int32, (2 * Y, Y), 0) % Y
    c = lax.broadcasted_iota(jnp.int32, (2 * Y, Y), 1)
    gap = r - c
    near = jnp.abs(gap) == 1
    far = jnp.abs(gap) == 2
    band[:, 0:Y] = jnp.where(gap == 0, -30.0, jnp.where(near, 16.0, jnp.where(far, -1.0, 0.0))).astype(BF16)
    sign = jnp.where(gap > 0, 1.0, -1.0)
    band[:, Y:2 * Y] = (jnp.where(near, 8.0, jnp.where(far, -1.0, 0.0)) * sign).astype(BF16)

    dest_row = meta[0:1, :]
    source_row = meta[1:2, :]
    fx_row = meta[2:3, :]
    fz_row = meta[3:4, :]
    fy_row = meta[4:5, :]
    target_row = meta[5:6, :]
    e_col = lax.broadcasted_iota(jnp.int32, (donors, donors), 0)
    e_row = lax.broadcasted_iota(jnp.int32, (donors, donors), 1)

    def to_col(row):
        return jnp.sum(jnp.where(e_col == e_row, row, 0.0), axis=1, keepdims=True)

    dest_col = to_col(dest_row)
    target_col = to_col(target_row)
    same = dest_col == dest_row
    rank_row = jnp.sum(jnp.where(same & (e_col < e_row), 1.0, 0.0), axis=0, keepdims=True)
    rank_col = jnp.sum(jnp.where(same & (e_row < e_col), 1.0, 0.0), axis=1, keepdims=True)
    position_row = dest_row * cap + rank_row
    lane = (lax.broadcasted_iota(jnp.int32, (donors, 128), 1) % cap).astype(F32)
    here = rank_col == lane
    for d in range(spans):
        picked = here & (dest_col == float(d))
        row = jnp.sum(jnp.where(picked, target_col + 1.0, 0.0), axis=0, keepdims=True) - 1.0
        tsend[d] = jnp.broadcast_to(row, (8, 128))

    def target_copy(peer, slot):
        return pltpu.make_async_remote_copy(
            src_ref=tsend.at[peer], dst_ref=trecv.at[slot], send_sem=ts_sem.at[peer],
            recv_sem=tr_sem.at[slot], device_id=(sx, peer), device_id_type=MESH)

    for k in range(1, spans):
        target_copy(lax.rem(me + k, spans), me).start()
    trecv[me] = tsend[me]

    @pl.loop(0, spans)
    def _(d):
        slot = (lax.broadcasted_iota(jnp.int32, (cap, donors), 0) + d * cap).astype(F32)
        mask = slot == position_row

        def pick(row):
            return jnp.sum(jnp.where(mask, row, 0.0), axis=1, keepdims=True)

        valid = pick(jnp.ones((1, donors), F32))
        source = pick(source_row).astype(jnp.int32)
        fx = pick(fx_row)
        fz = pick(fz_row)
        fy = pick(fy_row)
        wy[pl.ds(pl.multiple_of(d * cap, cap), cap), :] = jnp.broadcast_to(fy, (cap, Y))
        w00 = valid * (1.0 - fx) * (1.0 - fz)
        w10 = valid * fx * (1.0 - fz)
        w01 = valid * (1.0 - fx) * fz
        w11 = valid * fx * fz
        for j in range(X * Z // 256):
            col = lax.broadcasted_iota(jnp.int32, (cap, 256), 1) + j * 256 - source
            w = jnp.where(col == 0, w00, jnp.where(col == 1, w01, jnp.where(
                col == Z, w10, jnp.where(col == Z + 1, w11, 0.0))))
            high, low = split(w)
            a_high[pl.ds(pl.multiple_of(d * cap, cap), cap), j * 256:(j + 1) * 256] = high
            a_low[pl.ds(pl.multiple_of(d * cap, cap), cap), j * 256:(j + 1) * 256] = low

    for f in range(5):
        load(f).wait()

    def xcopy(s, side):
        first = 2 if side == 0 else X
        landed = X + 2 if side == 0 else 0
        peer = jnp.maximum(sx - 1, 0) if side == 0 else jnp.minimum(sx + 1, rows - 1)
        return pltpu.make_async_remote_copy(
            src_ref=q.at[s, :, pl.ds(first, 2), pl.ds(8, Z), :],
            dst_ref=q.at[s, :, pl.ds(landed, 2), pl.ds(8, Z), :],
            send_sem=xs_sem.at[side], recv_sem=xr_sem.at[s, side],
            device_id=(peer, me), device_id_type=MESH)

    def zcopy(s, side):
        peer = lax.rem(me + spans - 1, spans) if side == 0 else lax.rem(me + 1, spans)
        return pltpu.make_async_remote_copy(
            src_ref=zsend.at[side], dst_ref=zrecv.at[s, side],
            send_sem=zs_sem.at[side], recv_sem=zr_sem.at[s, side],
            device_id=(sx, peer), device_id_type=MESH)

    def tile_copy(s, f, peer, slot):
        return pltpu.make_async_remote_copy(
            src_ref=send.at[f, peer], dst_ref=recv.at[s, f, slot],
            send_sem=send_sem.at[f, peer], recv_sem=recv_sem.at[s, f, slot],
            device_id=(sx, peer), device_id_type=MESH)

    def land(s, f, target):
        @pl.loop(1, spans)
        def _(k):
            tile_copy(s, f, lax.rem(me + k, spans), lax.rem(me + k, spans)).wait_recv()
        scale = penalty_rate * time_step * jnp.where(s == 0, 1.0, jnp.where(s == 1, 0.25, 2.0 / 3.0))
        high, low = split(recv[s, f].reshape(slots, Y))
        rhs = jnp.concatenate([high, low], axis=1)
        group = 8 if (X - 8) % 8 == 0 else 4

        @pl.loop(0, (X - 8) // group)
        def _(g):
            part = landing[pl.ds(pl.multiple_of(g * group * Z, group * Z), group * Z), :]
            both = jnp.dot(part, rhs, preferred_element_type=F32)
            total = (both[:, 0:Y] + both[:, Y:2 * Y]) * scale
            for i in range(group):
                x = 6 + g * group + i
                q[target, f, x, 8:8 + Z, :] = q[target, f, x, 8:8 + Z, :] + total[i * Z:(i + 1) * Z]

    def interpolate(s, f):
        @pl.loop(0, X)
        def _(x):
            high, low = split(q[s, f, 2 + x, 8:8 + Z, :])
            at = pl.ds(pl.multiple_of(x * Z, Z), Z)
            qcat[at, 0:Y] = high
            qcat[at, Y:2 * Y] = low

        @pl.when(s > 0)
        def _():
            @pl.loop(1, spans)
            def _(k):
                tile_copy(s, f, lax.rem(me + k, spans), me).wait_send()

        block = 256

        @pl.loop(0, slots // block)
        def _(g):
            at = pl.ds(pl.multiple_of(g * block, block), block)
            both = jnp.dot(a_high[at, :], qcat[...], preferred_element_type=F32)
            rest = jnp.dot(a_low[at, :], qcat[:, 0:Y], preferred_element_type=F32)
            value = both[:, 0:Y] + both[:, Y:2 * Y] + rest
            lane = lax.broadcasted_iota(jnp.int32, (block, Y), 1)
            shifted = jnp.where(lane == Y - 1, 0.0, pltpu.roll(value, Y - 1, 1))
            value = value + wy[at, :] * (shifted - value)
            for i in range(block // cap):
                send[f, g * (block // cap) + i] = value[i * cap:(i + 1) * cap]

        @pl.loop(1, spans)
        def _(k):
            tile_copy(s, f, lax.rem(me + k, spans), me).start()
        recv[s, f, me] = send[f, me]

    def build_landing():
        for k in range(1, spans):
            peer = lax.rem(me + k, spans)
            target_copy(peer, peer).wait_recv()
        lane = lax.broadcasted_iota(jnp.int32, (8, 128), 1)
        for p in range(spans // 2):
            trow[:, p * 128:(p + 1) * 128] = jnp.where(lane < cap, trecv[2 * p], trecv[2 * p + 1])

        @pl.loop(0, X)
        def _(x):
            counted[x] = jnp.zeros((Z, Y), F32)

        @pl.loop(4, X - 4)
        def _(x):
            col = (lax.broadcasted_iota(jnp.int32, (Z, slots), 0) + x * Z).astype(F32)
            hit = jnp.where(col == trow[0:1, :], 1.0, 0.0)
            landing[pl.ds(pl.multiple_of((x - 4) * Z, Z), Z), :] = hit.astype(BF16)
            counted[x] = jnp.broadcast_to(jnp.sum(hit, axis=1, keepdims=True), (Z, Y))

    def stencil(s, target):
        ours = jnp.where(s == 0, 0.0, jnp.where(s == 1, 0.75, 1.0 / 3.0))
        kept = jnp.where(s == 0, 1.0, jnp.where(s == 1, 0.25, 2.0 / 3.0))
        rate = kept * time_step
        twelfth = rate * (1.0 / 12.0)
        nu = viscosity * twelfth
        tall = 16

        @pl.loop(0, X)
        def _(x):
            for f in range(5):
                high, low = split(q[s, f, 2 + x, 8:8 + Z, :])
                both = jnp.concatenate([high, low], axis=1)
                if f in (2, 4):
                    ybuf[f] = jnp.dot(both, band[...], preferred_element_type=F32)
                else:
                    ybuf[f, :, 0:Y] = jnp.dot(both, band[:, 0:Y], preferred_element_type=F32)

            @pl.loop(0, Z // tall)
            def _(t):
                z = t * tall
                zat = pl.ds(pl.multiple_of(z, tall), tall)
                stream_speed = flow[0, x, zat, :] * twelfth
                span_speed = flow[1, x, zat, :] * twelfth
                acoustic = flow[2, x, zat, :] * twelfth
                shear = flow[3, x, zat, :] * rate
                held = kept - (penalty_rate * rate) * counted[x, zat, :]
                result, dx, dz, mid = [], [], [], []
                for f in range(5):
                    def at(i, j):
                        return q[s, f, x + 2 + i, pl.ds(z + 8 + j, tall), :]
                    m = q[s, f, x + 2, pl.ds(pl.multiple_of(z + 8, 8), tall), :]
                    x0, x1, x3, x4 = at(-2, 0), at(-1, 0), at(1, 0), at(2, 0)
                    z0, z1, z3, z4 = at(0, -2), at(0, -1), at(0, 1), at(0, 2)
                    gx = 8.0 * (x3 - x1) - (x4 - x0)
                    gz = 8.0 * (z3 - z1) - (z4 - z0)
                    lap = 16.0 * ((x1 + x3) + (z1 + z3)) - ((x0 + x4) + (z0 + z4)) - 60.0 * m
                    lap = lap + ybuf[f, zat, 0:Y]
                    old = q[0, f, x + 2, pl.ds(pl.multiple_of(z + 8, 8), tall), :]
                    result.append(ours * old + held * m + nu * lap - stream_speed * gx - span_speed * gz)
                    dx.append(gx)
                    dz.append(gz)
                    mid.append(m)
                result[1] = result[1] - acoustic * dx[4] - shear * mid[2]
                result[2] = result[2] - acoustic * ybuf[4, zat, Y:2 * Y]
                result[3] = result[3] - acoustic * dz[4]
                result[4] = result[4] - acoustic * (dx[1] + ybuf[2, zat, Y:2 * Y] + dz[3])
                for f in range(5):
                    q[target, f, x + 2, pl.ds(pl.multiple_of(z + 8, 8), tall), :] = result[f]

    @pl.loop(0, 3)
    def _(s):
        @pl.when(sx > 0)
        def _():
            xcopy(s, 0).start()

        @pl.when(sx < rows - 1)
        def _():
            xcopy(s, 1).start()

        for f in range(5):
            @pl.loop(0, X)
            def _(x):
                at = pl.ds((f * X + x) * 2, 2)
                zsend[0, at, :] = q[s, f, x + 2, 8:10, :]
                zsend[1, at, :] = q[s, f, x + 2, Z + 6:Z + 8, :]
        zcopy(s, 0).start()
        zcopy(s, 1).start()

        @pl.loop(0, 5)
        def _(f):
            @pl.when(s > 0)
            def _():
                land(s - 1, f, s)
            interpolate(s, f)

        @pl.when(s == 0)
        def _():
            build_landing()
            flow_load.wait()

        zcopy(s, 0).wait()
        zcopy(s, 1).wait()
        for f in range(5):
            @pl.loop(0, X)
            def _(x):
                at = pl.ds((f * X + x) * 2, 2)
                q[s, f, x + 2, Z + 8:Z + 10, :] = zrecv[s, 0, at, :]
                q[s, f, x + 2, 6:8, :] = zrecv[s, 1, at, :]

        @pl.when(sx > 0)
        def _():
            xcopy(s, 0).wait_send()
            xcopy(s, 1).wait_recv()

        @pl.when(sx < rows - 1)
        def _():
            xcopy(s, 1).wait_send()
            xcopy(s, 0).wait_recv()

        stencil(s, lax.rem(s + 1, 3))

    def store(f):
        return pltpu.make_async_copy(
            q.at[0, f, pl.ds(2, X), pl.ds(8, Z), :], out.at[f], out_sem.at[f])

    @pl.loop(0, 5)
    def _(f):
        land(2, f, 0)
        store(f).start()

    @pl.loop(0, 5)
    def _(f):
        store(f).wait()

        @pl.loop(1, spans)
        def _(k):
            tile_copy(2, f, lax.rem(me + k, spans), me).wait_send()

    for k in range(1, spans):
        target_copy(lax.rem(me + k, spans), me).wait_send()


def body(rows, spans, perturbation, base_flow, donor_stream, donor_span, donor_weights,
         donor_receiver, target_stream, target_span):
    _, X, Z, Y = perturbation.shape
    donors = donor_stream.shape[1]
    cap = donors // 4
    slots = spans * cap
    assert Y == 128 and 2 * cap == 128 and rows > 2
    source = donor_stream * Z + donor_span
    target = target_stream * Z + target_span
    zero = jnp.zeros_like(donor_weights[0])
    meta = jnp.concatenate(
        [donor_receiver.astype(F32), source.astype(F32), donor_weights[0], donor_weights[1],
         donor_weights[2], target.astype(F32), zero, zero], axis=0)
    dma = pltpu.SemaphoreType.DMA
    return pl.pallas_call(
        functools.partial(kernel, rows, spans, X, Z, donors, cap),
        out_shape=jax.ShapeDtypeStruct(perturbation.shape, F32),
        in_specs=[pl.BlockSpec(memory_space=pl.ANY), pl.BlockSpec(memory_space=pl.ANY),
                  pl.BlockSpec(memory_space=pltpu.VMEM)],
        out_specs=pl.BlockSpec(memory_space=pl.ANY),
        scratch_shapes=[
            pltpu.VMEM((3, 5, X + 4, Z + 16, Y), F32),
            pltpu.VMEM((4, X, Z, Y), F32),
            pltpu.VMEM((5, spans, cap, Y), F32),
            pltpu.VMEM((3, 5, spans, cap, Y), F32),
            pltpu.VMEM((2, 5 * X * 2, Y), F32),
            pltpu.VMEM((3, 2, 5 * X * 2, Y), F32),
            pltpu.VMEM((spans, 8, 128), F32),
            pltpu.VMEM((spans, 8, 128), F32),
            pltpu.VMEM((slots, X * Z), BF16),
            pltpu.VMEM((slots, X * Z), BF16),
            pltpu.VMEM((slots, Y), F32),
            pltpu.VMEM(((X - 8) * Z, slots), BF16),
            pltpu.VMEM((X, Z, Y), F32),
            pltpu.VMEM((8, slots), F32),
            pltpu.VMEM((X * Z, 2 * Y), BF16),
            pltpu.VMEM((2 * Y, 2 * Y), BF16),
            pltpu.VMEM((5, Z, 2 * Y), F32),
            dma((6,)), dma((5,)), dma((5, spans)), dma((3, 5, spans)),
            dma((2,)), dma((3, 2)), dma((2,)), dma((3, 2)), dma((spans,)), dma((spans,)),
        ],
        compiler_params=pltpu.CompilerParams(
            collective_id=0, has_side_effects=True, vmem_limit_bytes=63 * 2**20),
    )(perturbation, base_flow, meta)


def solution(mesh):
    in_specs = (
        P(None, "stream", "span", None),
        P(None, "stream", "span", None),
        P("stream", "span"),
        P("stream", "span"),
        P(None, "stream", "span"),
        P("stream", "span"),
        P("stream", "span"),
        P("stream", "span"),
    )
    out_specs = P(None, "stream", "span", None)
    part = functools.partial(body, mesh.shape["stream"], mesh.shape["span"])
    return jax.shard_map(part, mesh=mesh, in_specs=in_specs, out_specs=out_specs, check_vma=False)
```

profile of v0, /device:TPU:9, one launch (start us, length us, event | category | flops | bytes accessed | tf_op | source)
XLA Modules:
  0.0 127.2 jit_solution(2637979099194172911)
XLA Ops:
  0.0 0.7 convert_element_type.9
  0.7 0.7 add_convert_fusion
  1.4 0.7 slice_bitcast_fusion
  2.1 0.6 concatenate.7.meta
  2.7 118.8 %shard_map.82 = f32[5,32,64,128]{3,2,1,0:T(8,128)} custom-call(f32[5,32,64,128]{3,2,1,0:T(8,128)} %pert.1, f32[4,32,64,128]{3,2,1,0:T(8,128)} %flow_in.1, f32[8,256]{1,0:T(8,128)} %concatenate.7.meta), custom_call_target="tpu_custom_call" | custom-call | tf_op jit(solution)/shard_map/pallas_call | solution.py:367
  121.5 5.7 %copy.10 = f32[5,32,64,128]{3,2,1,0:T(8,128)} copy(f32[5,32,64,128]{3,2,1,0:T(8,128)} %shard_map.82) | data formatting | bytes 10485760
  (1 shorter events, 0.0 us)
where the time goes:
time: 127 us
  Pallas kernels  119 us (94%)
  local copies, waits for them, and re-layouts  7.03 us (6%)
  other arithmetic  1.41 us (1%)
    pallas_call x1, Pallas kernels, body(): pl.pallas_call(functools.partial(kernel, rows, spans, X, Z, donors, cap),...  119 us
    unnamed x1, local copies, waits for them, and re-layouts  5.7 us

commit v1 on v0

--- a/solution.py
+++ b/solution.py
@@ -23,7 +23,7 @@
 
 def kernel(
     rows, spans, X, Z, donors, cap,
-    pert, flow_in, meta, out,
+    pert, flow_in, d_stream, d_span, d_weights, d_receiver, t_stream, t_span, out,
     q, flow, send, recv, zsend, zrecv, tsend, trecv,
     a_high, a_low, wy, landing, counted, trow, qcat, band, ybuf,
     load_sem, out_sem, send_sem, recv_sem, xs_sem, xr_sem, zs_sem, zr_sem, ts_sem, tr_sem,
@@ -71,12 +71,12 @@
     sign = jnp.where(gap > 0, 1.0, -1.0)
     band[:, Y:2 * Y] = (jnp.where(near, 8.0, jnp.where(far, -1.0, 0.0)) * sign).astype(BF16)
 
-    dest_row = meta[0:1, :]
-    source_row = meta[1:2, :]
-    fx_row = meta[2:3, :]
-    fz_row = meta[3:4, :]
-    fy_row = meta[4:5, :]
-    target_row = meta[5:6, :]
+    dest_row = d_receiver[...].astype(F32)
+    source_row = (d_stream[...] * Z + d_span[...]).astype(F32)
+    fx_row = d_weights[0]
+    fz_row = d_weights[1]
+    fy_row = d_weights[2]
+    target_row = (t_stream[...] * Z + t_span[...]).astype(F32)
     e_col = lax.broadcasted_iota(jnp.int32, (donors, donors), 0)
     e_row = lax.broadcasted_iota(jnp.int32, (donors, donors), 1)
 
@@ -104,6 +104,46 @@
     for k in range(1, spans):
         target_copy(lax.rem(me + k, spans), me).start()
     trecv[me] = tsend[me]
+
+    for f in range(5):
+        load(f).wait()
+
+    def xcopy(s, side):
+        first = 2 if side == 0 else X
+        landed = X + 2 if side == 0 else 0
+        peer = jnp.maximum(sx - 1, 0) if side == 0 else jnp.minimum(sx + 1, rows - 1)
+        return pltpu.make_async_remote_copy(
+            src_ref=q.at[s, :, pl.ds(first, 2), pl.ds(8, Z), :],
+            dst_ref=q.at[s, :, pl.ds(landed, 2), pl.ds(8, Z), :],
+            send_sem=xs_sem.at[side], recv_sem=xr_sem.at[s, side],
+            device_id=(peer, me), device_id_type=MESH)
+
+    def zcopy(s, side):
+        peer = lax.rem(me + spans - 1, spans) if side == 0 else lax.rem(me + 1, spans)
+        return pltpu.make_async_remote_copy(
+            src_ref=zsend.at[side], dst_ref=zrecv.at[s, side],
+            send_sem=zs_sem.at[side], recv_sem=zr_sem.at[s, side],
+            device_id=(sx, peer), device_id_type=MESH)
+
+    def send_halos(s):
+        @pl.when(sx > 0)
+        def _():
+            xcopy(s, 0).start()
+
+        @pl.when(sx < rows - 1)
+        def _():
+            xcopy(s, 1).start()
+
+        for f in range(5):
+            @pl.loop(0, X)
+            def _(x):
+                at = pl.ds((f * X + x) * 2, 2)
+                zsend[0, at, :] = q[s, f, x + 2, 8:10, :]
+                zsend[1, at, :] = q[s, f, x + 2, Z + 6:Z + 8, :]
+        zcopy(s, 0).start()
+        zcopy(s, 1).start()
+
+    send_halos(0)
 
     @pl.loop(0, spans)
     def _(d):
@@ -131,26 +171,6 @@
             a_high[pl.ds(pl.multiple_of(d * cap, cap), cap), j * 256:(j + 1) * 256] = high
             a_low[pl.ds(pl.multiple_of(d * cap, cap), cap), j * 256:(j + 1) * 256] = low
 
-    for f in range(5):
-        load(f).wait()
-
-    def xcopy(s, side):
-        first = 2 if side == 0 else X
-        landed = X + 2 if side == 0 else 0
-        peer = jnp.maximum(sx - 1, 0) if side == 0 else jnp.minimum(sx + 1, rows - 1)
-        return pltpu.make_async_remote_copy(
-            src_ref=q.at[s, :, pl.ds(first, 2), pl.ds(8, Z), :],
-            dst_ref=q.at[s, :, pl.ds(landed, 2), pl.ds(8, Z), :],
-            send_sem=xs_sem.at[side], recv_sem=xr_sem.at[s, side],
-            device_id=(peer, me), device_id_type=MESH)
-
-    def zcopy(s, side):
-        peer = lax.rem(me + spans - 1, spans) if side == 0 else lax.rem(me + 1, spans)
-        return pltpu.make_async_remote_copy(
-            src_ref=zsend.at[side], dst_ref=zrecv.at[s, side],
-            send_sem=zs_sem.at[side], recv_sem=zr_sem.at[s, side],
-            device_id=(sx, peer), device_id_type=MESH)
-
     def tile_copy(s, f, peer, slot):
         return pltpu.make_async_remote_copy(
             src_ref=send.at[f, peer], dst_ref=recv.at[s, f, slot],
@@ -237,13 +257,11 @@
 
         @pl.loop(0, X)
         def _(x):
+            pairs = []
             for f in range(5):
-                high, low = split(q[s, f, 2 + x, 8:8 + Z, :])
-                both = jnp.concatenate([high, low], axis=1)
-                if f in (2, 4):
-                    ybuf[f] = jnp.dot(both, band[...], preferred_element_type=F32)
-                else:
-                    ybuf[f, :, 0:Y] = jnp.dot(both, band[:, 0:Y], preferred_element_type=F32)
+                pairs.append(jnp.concatenate(split(q[s, f, 2 + x, 8:8 + Z, :]), axis=1))
+            wall = jnp.dot(jnp.concatenate(pairs, axis=0), band[...], preferred_element_type=F32)
+            ybuf[...] = wall.reshape(5, Z, 2 * Y)
 
             @pl.loop(0, Z // tall)
             def _(t):
@@ -279,23 +297,6 @@
 
     @pl.loop(0, 3)
     def _(s):
-        @pl.when(sx > 0)
-        def _():
-            xcopy(s, 0).start()
-
-        @pl.when(sx < rows - 1)
-        def _():
-            xcopy(s, 1).start()
-
-        for f in range(5):
-            @pl.loop(0, X)
-            def _(x):
-                at = pl.ds((f * X + x) * 2, 2)
-                zsend[0, at, :] = q[s, f, x + 2, 8:10, :]
-                zsend[1, at, :] = q[s, f, x + 2, Z + 6:Z + 8, :]
-        zcopy(s, 0).start()
-        zcopy(s, 1).start()
-
         @pl.loop(0, 5)
         def _(f):
             @pl.when(s > 0)
@@ -329,6 +330,10 @@
 
         stencil(s, lax.rem(s + 1, 3))
 
+        @pl.when(s < 2)
+        def _():
+            send_halos(s + 1)
+
     def store(f):
         return pltpu.make_async_copy(
             q.at[0, f, pl.ds(2, X), pl.ds(8, Z), :], out.at[f], out_sem.at[f])
@@ -357,18 +362,12 @@
     cap = donors // 4
     slots = spans * cap
     assert Y == 128 and 2 * cap == 128 and rows > 2
-    source = donor_stream * Z + donor_span
-    target = target_stream * Z + target_span
-    zero = jnp.zeros_like(donor_weights[0])
-    meta = jnp.concatenate(
-        [donor_receiver.astype(F32), source.astype(F32), donor_weights[0], donor_weights[1],
-         donor_weights[2], target.astype(F32), zero, zero], axis=0)
     dma = pltpu.SemaphoreType.DMA
     return pl.pallas_call(
         functools.partial(kernel, rows, spans, X, Z, donors, cap),
         out_shape=jax.ShapeDtypeStruct(perturbation.shape, F32),
         in_specs=[pl.BlockSpec(memory_space=pl.ANY), pl.BlockSpec(memory_space=pl.ANY),
-                  pl.BlockSpec(memory_space=pltpu.VMEM)],
+                  *[pl.BlockSpec(memory_space=pltpu.VMEM)] * 6],
         out_specs=pl.BlockSpec(memory_space=pl.ANY),
         scratch_shapes=[
             pltpu.VMEM((3, 5, X + 4, Z + 16, Y), F32),
@@ -393,7 +392,8 @@
         ],
         compiler_params=pltpu.CompilerParams(
             collective_id=0, has_side_effects=True, vmem_limit_bytes=63 * 2**20),
-    )(perturbation, base_flow, meta)
+    )(perturbation, base_flow, donor_stream, donor_span, donor_weights, donor_receiver,
+      target_stream, target_span)
 
 
 def solution(mesh):

time: 127 us -> 117 us (0.921)
  Pallas kernels: 119 us -> 111 us
  other arithmetic: 1.41 us -> 0 us
  local copies, waits for them, and re-layouts: 7.03 us -> 5.7 us
    pallas_call x1, Pallas kernels: 119 us -> 111 us  [body(): pl.pallas_call(functools.partial(kernel, rows, spans, X, Z, donors, cap),...]
    convert_element_type x2 -> x0, other arithmetic: 1.41 us -> none  [the longest x1 0.73 us: body(): target.astype(F32)]
where the time goes in v1:
time: 117 us
  Pallas kernels  111 us (95%)
  local copies, waits for them, and re-layouts  5.7 us (5%)
    pallas_call x1, Pallas kernels, body(): pl.pallas_call(functools.partial(kernel, rows, spans, X, Z, donors, cap),...  111 us
    unnamed x1, local copies, waits for them, and re-layouts  5.7 us

profile of v1, /device:TPU:9, one launch (start us, length us, event | category | flops | bytes accessed | tf_op | source)
XLA Modules:
  0.0 116.7 jit_solution(6023163320839348164)
XLA Ops:
  0.0 111.0 %shard_map.82 = f32[5,32,64,128]{3,2,1,0:T(8,128)} custom-call(f32[5,32,64,128]{3,2,1,0:T(8,128)} %pert.1, f32[4,32,64,128]{3,2,1,0:T(8,128)} %flow_in.1, s32[1,256]{1,0:T(1,128)} %d_stream.1, s32[1,256]{1,0:T(1,128)} %d_span.1, f32[3,1,256]{2,1,0:T(1,128)} %d_weights.1, s32[1,256]{1,0:T(1,128)} %d_receiver.1, s32[1,256]{1,0:T(1,128)} %t_stream.1, ...), custom_call_target="tpu_custom_call" | custom-call | tf_op jit(solution)/shard_map/pallas_call | solution.py:366
  111.0 5.7 %copy.10 = f32[5,32,64,128]{3,2,1,0:T(8,128)} copy(f32[5,32,64,128]{3,2,1,0:T(8,128)} %shard_map.82) | data formatting | bytes 10485760

commit v2 on v1

--- a/solution.py
+++ b/solution.py
@@ -25,13 +25,15 @@
     rows, spans, X, Z, donors, cap,
     pert, flow_in, d_stream, d_span, d_weights, d_receiver, t_stream, t_span, out,
     q, flow, send, recv, zsend, zrecv, tsend, trecv,
-    a_high, a_low, wy, landing, counted, trow, qcat, band, ybuf,
+    donor, wy, landing, counted, trow, qcat, band, ybuf,
     load_sem, out_sem, send_sem, recv_sem, xs_sem, xr_sem, zs_sem, zr_sem, ts_sem, tr_sem,
 ):
     sx = lax.axis_index("stream")
     me = lax.axis_index("span")
     Y = 128
     slots = spans * cap
+    block = 256
+    step = 4
 
     def load(f):
         return pltpu.make_async_copy(
@@ -134,12 +136,14 @@
         def _():
             xcopy(s, 1).start()
 
-        for f in range(5):
-            @pl.loop(0, X)
-            def _(x):
-                at = pl.ds((f * X + x) * 2, 2)
-                zsend[0, at, :] = q[s, f, x + 2, 8:10, :]
-                zsend[1, at, :] = q[s, f, x + 2, Z + 6:Z + 8, :]
+        @pl.loop(0, X // step)
+        def _(xo):
+            for f in range(5):
+                for i in range(step):
+                    x = xo * step + i
+                    at = pl.ds((f * X + x) * 2, 2)
+                    zsend[0, at, :] = q[s, f, x + 2, 8:10, :]
+                    zsend[1, at, :] = q[s, f, x + 2, Z + 6:Z + 8, :]
         zcopy(s, 0).start()
         zcopy(s, 1).start()
 
@@ -149,6 +153,7 @@
     def _(d):
         slot = (lax.broadcasted_iota(jnp.int32, (cap, donors), 0) + d * cap).astype(F32)
         mask = slot == position_row
+        first = (d // (block // cap)) * (2 * block) + (d % (block // cap)) * cap
 
         def pick(row):
             return jnp.sum(jnp.where(mask, row, 0.0), axis=1, keepdims=True)
@@ -168,8 +173,8 @@
             w = jnp.where(col == 0, w00, jnp.where(col == 1, w01, jnp.where(
                 col == Z, w10, jnp.where(col == Z + 1, w11, 0.0))))
             high, low = split(w)
-            a_high[pl.ds(pl.multiple_of(d * cap, cap), cap), j * 256:(j + 1) * 256] = high
-            a_low[pl.ds(pl.multiple_of(d * cap, cap), cap), j * 256:(j + 1) * 256] = low
+            donor[pl.ds(pl.multiple_of(first, cap), cap), j * 256:(j + 1) * 256] = high
+            donor[pl.ds(pl.multiple_of(first + block, cap), cap), j * 256:(j + 1) * 256] = low
 
     def tile_copy(s, f, peer, slot):
         return pltpu.make_async_remote_copy(
@@ -196,12 +201,14 @@
                 q[target, f, x, 8:8 + Z, :] = q[target, f, x, 8:8 + Z, :] + total[i * Z:(i + 1) * Z]
 
     def interpolate(s, f):
-        @pl.loop(0, X)
-        def _(x):
-            high, low = split(q[s, f, 2 + x, 8:8 + Z, :])
-            at = pl.ds(pl.multiple_of(x * Z, Z), Z)
-            qcat[at, 0:Y] = high
-            qcat[at, Y:2 * Y] = low
+        @pl.loop(0, X // step)
+        def _(xo):
+            for i in range(step):
+                x = xo * step + i
+                high, low = split(q[s, f, 2 + x, 8:8 + Z, :])
+                at = pl.ds(pl.multiple_of(x * Z, Z), Z)
+                qcat[at, 0:Y] = high
+                qcat[at, Y:2 * Y] = low
 
         @pl.when(s > 0)
         def _():
@@ -209,14 +216,12 @@
             def _(k):
                 tile_copy(s, f, lax.rem(me + k, spans), me).wait_send()
 
-        block = 256
-
         @pl.loop(0, slots // block)
         def _(g):
             at = pl.ds(pl.multiple_of(g * block, block), block)
-            both = jnp.dot(a_high[at, :], qcat[...], preferred_element_type=F32)
-            rest = jnp.dot(a_low[at, :], qcat[:, 0:Y], preferred_element_type=F32)
-            value = both[:, 0:Y] + both[:, Y:2 * Y] + rest
+            pair = pl.ds(pl.multiple_of(g * (2 * block), 2 * block), 2 * block)
+            both = jnp.dot(donor[pair, :], qcat[...], preferred_element_type=F32)
+            value = both[0:block, 0:Y] + both[0:block, Y:2 * Y] + both[block:2 * block, 0:Y]
             lane = lax.broadcasted_iota(jnp.int32, (block, Y), 1)
             shifted = jnp.where(lane == Y - 1, 0.0, pltpu.roll(value, Y - 1, 1))
             value = value + wy[at, :] * (shifted - value)
@@ -255,17 +260,20 @@
         nu = viscosity * twelfth
         tall = 16
 
-        @pl.loop(0, X)
-        def _(x):
-            pairs = []
-            for f in range(5):
-                pairs.append(jnp.concatenate(split(q[s, f, 2 + x, 8:8 + Z, :]), axis=1))
-            wall = jnp.dot(jnp.concatenate(pairs, axis=0), band[...], preferred_element_type=F32)
-            ybuf[...] = wall.reshape(5, Z, 2 * Y)
-
-            @pl.loop(0, Z // tall)
+        @pl.loop(0, X // step)
+        def _(xo):
+            for i in range(step):
+                pairs = []
+                for f in range(5):
+                    pairs.append(jnp.concatenate(split(q[s, f, 2 + xo * step + i, 8:8 + Z, :]), axis=1))
+                wall = jnp.dot(jnp.concatenate(pairs, axis=0), band[...], preferred_element_type=F32)
+                ybuf[i] = wall.reshape(5, Z, 2 * Y)
+
+            @pl.loop(0, step * (Z // tall))
             def _(t):
-                z = t * tall
+                row = t // (Z // tall)
+                x = xo * step + row
+                z = (t % (Z // tall)) * tall
                 zat = pl.ds(pl.multiple_of(z, tall), tall)
                 stream_speed = flow[0, x, zat, :] * twelfth
                 span_speed = flow[1, x, zat, :] * twelfth
@@ -282,16 +290,16 @@
                     gx = 8.0 * (x3 - x1) - (x4 - x0)
                     gz = 8.0 * (z3 - z1) - (z4 - z0)
                     lap = 16.0 * ((x1 + x3) + (z1 + z3)) - ((x0 + x4) + (z0 + z4)) - 60.0 * m
-                    lap = lap + ybuf[f, zat, 0:Y]
+                    lap = lap + ybuf[row, f, zat, 0:Y]
                     old = q[0, f, x + 2, pl.ds(pl.multiple_of(z + 8, 8), tall), :]
                     result.append(ours * old + held * m + nu * lap - stream_speed * gx - span_speed * gz)
                     dx.append(gx)
                     dz.append(gz)
                     mid.append(m)
                 result[1] = result[1] - acoustic * dx[4] - shear * mid[2]
-                result[2] = result[2] - acoustic * ybuf[4, zat, Y:2 * Y]
+                result[2] = result[2] - acoustic * ybuf[row, 4, zat, Y:2 * Y]
                 result[3] = result[3] - acoustic * dz[4]
-                result[4] = result[4] - acoustic * (dx[1] + ybuf[2, zat, Y:2 * Y] + dz[3])
+                result[4] = result[4] - acoustic * (dx[1] + ybuf[row, 2, zat, Y:2 * Y] + dz[3])
                 for f in range(5):
                     q[target, f, x + 2, pl.ds(pl.multiple_of(z + 8, 8), tall), :] = result[f]
 
@@ -311,12 +319,14 @@
 
         zcopy(s, 0).wait()
         zcopy(s, 1).wait()
-        for f in range(5):
-            @pl.loop(0, X)
-            def _(x):
-                at = pl.ds((f * X + x) * 2, 2)
-                q[s, f, x + 2, Z + 8:Z + 10, :] = zrecv[s, 0, at, :]
-                q[s, f, x + 2, 6:8, :] = zrecv[s, 1, at, :]
+        @pl.loop(0, X // step)
+        def _(xo):
+            for f in range(5):
+                for i in range(step):
+                    x = xo * step + i
+                    at = pl.ds((f * X + x) * 2, 2)
+                    q[s, f, x + 2, Z + 8:Z + 10, :] = zrecv[s, 0, at, :]
+                    q[s, f, x + 2, 6:8, :] = zrecv[s, 1, at, :]
 
         @pl.when(sx > 0)
         def _():
@@ -361,7 +371,7 @@
     donors = donor_stream.shape[1]
     cap = donors // 4
     slots = spans * cap
-    assert Y == 128 and 2 * cap == 128 and rows > 2
+    assert Y == 128 and 2 * cap == 128 and rows > 2 and X % 4 == 0
     dma = pltpu.SemaphoreType.DMA
     return pl.pallas_call(
         functools.partial(kernel, rows, spans, X, Z, donors, cap),
@@ -378,15 +388,14 @@
             pltpu.VMEM((3, 2, 5 * X * 2, Y), F32),
             pltpu.VMEM((spans, 8, 128), F32),
             pltpu.VMEM((spans, 8, 128), F32),
-            pltpu.VMEM((slots, X * Z), BF16),
-            pltpu.VMEM((slots, X * Z), BF16),
+            pltpu.VMEM((2 * slots, X * Z), BF16),
             pltpu.VMEM((slots, Y), F32),
             pltpu.VMEM(((X - 8) * Z, slots), BF16),
             pltpu.VMEM((X, Z, Y), F32),
             pltpu.VMEM((8, slots), F32),
             pltpu.VMEM((X * Z, 2 * Y), BF16),
             pltpu.VMEM((2 * Y, 2 * Y), BF16),
-            pltpu.VMEM((5, Z, 2 * Y), F32),
+            pltpu.VMEM((4, 5, Z, 2 * Y), F32),
             dma((6,)), dma((5,)), dma((5, spans)), dma((3, 5, spans)),
             dma((2,)), dma((3, 2)), dma((2,)), dma((3, 2)), dma((spans,)), dma((spans,)),
         ],

time: 117 us -> 117 us (level)
  no operation moved by 1% of the time
where the time goes in v2:
time: 117 us; the launch traced here: 116 us
  Pallas kernels  111 us (95%)
  local copies, waits for them, and re-layouts  5.7 us (5%)
    pallas_call x1, Pallas kernels, body(): pl.pallas_call(functools.partial(kernel, rows, spans, X, Z, donors, cap),...  111 us
    unnamed x1, local copies, waits for them, and re-layouts  5.7 us

profile of v2, /device:TPU:9, one launch (start us, length us, event | category | flops | bytes accessed | tf_op | source)
XLA Modules:
  0.0 116.5 jit_solution(7257672111210158469)
XLA Ops:
  0.0 110.8 %shard_map.82 = f32[5,32,64,128]{3,2,1,0:T(8,128)} custom-call(f32[5,32,64,128]{3,2,1,0:T(8,128)} %pert.1, f32[4,32,64,128]{3,2,1,0:T(8,128)} %flow_in.1, s32[1,256]{1,0:T(1,128)} %d_stream.1, s32[1,256]{1,0:T(1,128)} %d_span.1, f32[3,1,256]{2,1,0:T(1,128)} %d_weights.1, s32[1,256]{1,0:T(1,128)} %d_receiver.1, s32[1,256]{1,0:T(1,128)} %t_stream.1, ...), custom_call_target="tpu_custom_call" | custom-call | tf_op jit(solution)/shard_map/pallas_call | solution.py:376
  110.8 5.7 %copy.10 = f32[5,32,64,128]{3,2,1,0:T(8,128)} copy(f32[5,32,64,128]{3,2,1,0:T(8,128)} %shard_map.82) | data formatting | bytes 10485760

commit v3 on v2

--- a/solution.py
+++ b/solution.py
@@ -365,6 +365,22 @@
         target_copy(lax.rem(me + k, spans), me).wait_send()
 
 
+def deliver(state, out, held, in_sem, out_sem):
+    parts, half = 2, state.shape[1] // 2
+
+    def pieces(ref, k):
+        return ref.at[k // parts, pl.ds((k % parts) * half, half)]
+
+    total = state.shape[0] * parts
+    for k in range(total):
+        pltpu.make_async_copy(pieces(state, k), pieces(held, k), in_sem.at[k]).start()
+    for k in range(total):
+        pltpu.make_async_copy(pieces(state, k), pieces(held, k), in_sem.at[k]).wait()
+        pltpu.make_async_copy(pieces(held, k), pieces(out, k), out_sem.at[k]).start()
+    for k in range(total):
+        pltpu.make_async_copy(pieces(held, k), pieces(out, k), out_sem.at[k]).wait()
+
+
 def body(rows, spans, perturbation, base_flow, donor_stream, donor_span, donor_weights,
          donor_receiver, target_stream, target_span):
     _, X, Z, Y = perturbation.shape
@@ -373,7 +389,7 @@
     slots = spans * cap
     assert Y == 128 and 2 * cap == 128 and rows > 2 and X % 4 == 0
     dma = pltpu.SemaphoreType.DMA
-    return pl.pallas_call(
+    finished = pl.pallas_call(
         functools.partial(kernel, rows, spans, X, Z, donors, cap),
         out_shape=jax.ShapeDtypeStruct(perturbation.shape, F32),
         in_specs=[pl.BlockSpec(memory_space=pl.ANY), pl.BlockSpec(memory_space=pl.ANY),
@@ -403,6 +419,14 @@
             collective_id=0, has_side_effects=True, vmem_limit_bytes=63 * 2**20),
     )(perturbation, base_flow, donor_stream, donor_span, donor_weights, donor_receiver,
       target_stream, target_span)
+    return pl.pallas_call(
+        deliver,
+        out_shape=jax.ShapeDtypeStruct(perturbation.shape, F32),
+        in_specs=[pl.BlockSpec(memory_space=pl.ANY)],
+        out_specs=pl.BlockSpec(memory_space=pl.ANY),
+        scratch_shapes=[pltpu.VMEM(perturbation.shape, F32), dma((10,)), dma((10,))],
+        compiler_params=pltpu.CompilerParams(vmem_limit_bytes=63 * 2**20),
+    )(finished)
 
 
 def solution(mesh):

time: 117 us -> 116 us (level)
  local copies, waits for them, and re-layouts: 5.7 us -> 0 us
  Pallas kernels: 111 us -> 115 us
    unnamed x1 -> x0, local copies, waits for them, and re-layouts: 5.7 us -> none
    pallas_call x0 -> x1, Pallas kernels: none -> 4.71 us  [body(): pl.pallas_call(deliver, out_shape=jax.ShapeDtypeStruct(perturbation.shape...]
where the time goes in v3:
time: 116 us; the launch traced here: 115 us
  Pallas kernels  115 us (99%)
    pallas_call x1, Pallas kernels, body(): pl.pallas_call(functools.partial(kernel, rows, spans, X, Z, donors, cap),...  111 us
    pallas_call x1, Pallas kernels, body(): pl.pallas_call(deliver, out_shape=jax.ShapeDtypeStruct(perturbation.shape...  4.71 us

profile of v3, /device:TPU:9, one launch (start us, length us, event | category | flops | bytes accessed | tf_op | source)
XLA Modules:
  0.0 115.5 jit_solution(984436802258492899)
XLA Ops:
  0.0 110.8 %shard_map.82.state = f32[5,32,64,128]{3,2,1,0:T(8,128)} custom-call(f32[5,32,64,128]{3,2,1,0:T(8,128)} %pert.1, f32[4,32,64,128]{3,2,1,0:T(8,128)} %flow_in.1, s32[1,256]{1,0:T(1,128)} %d_stream.1, s32[1,256]{1,0:T(1,128)} %d_span.1, f32[3,1,256]{2,1,0:T(1,128)} %d_weights.1, s32[1,256]{1,0:T(1,128)} %d_receiver.1, s32[1,256]{1,0:T(1,128)} %t_stream.1, ...), custom_call_target="tpu_custom_call" | custom-call | tf_op jit(solution)/shard_map/pallas_call | solution.py:392
  110.8 4.7 %shard_map.83 = f32[5,32,64,128]{3,2,1,0:T(8,128)} custom-call(f32[5,32,64,128]{3,2,1,0:T(8,128)} %shard_map.82.state), custom_call_target="tpu_custom_call" | custom-call | tf_op jit(solution)/shard_map/pallas_call | solution.py:422
